TPU v7x, 512 devices: a whole 4x8x8 slice. The times are simulated.
512 devices in a mesh: src: 8 (over x, y_lo), gx: 16 (over z, core), gy: 4 (over y_hi).
Axes of the slice: x: 4, y: 8 (y_hi: 4, y_lo: 2; y = y_hi * 2 + y_lo), z: 8, core: 2. Of those that a mesh axis runs over, the one named last changes fastest.
Arguments:
- warm_potential: float32 [32, 64, 128, 128], P('src', 'gx', 'gy'), may hold values from -3 to 3
- warm_adjoint: float32 [32, 64, 128, 128], P('src', 'gx', 'gy'), may hold values from -3 to 3
- conductivity: float32 [64, 128, 128], P('gx', 'gy', 'src'), may hold values from 0.2 to 5
- electrodes: int32 [32, 2], replicated, may hold values from 0 to 8191
- receivers: int32 [128, 2], replicated, may hold values from 0 to 8191
- observed: float32 [32, 128], replicated, may hold values from -6 to 6
- source_order: int32 [32], replicated, may hold values from 0 to 31, each once
Outputs:
- gradient: float32 [64, 128, 128], P('gx', 'gy', 'src')
Inputs may be any that keep to these rules, and one draw needn't show every extreme that they name: `electrodes`: entries number surface cells as x * 128 + y. `receivers`: entries number surface cells as x * 128 + y.
All inputs are finite; a program needn't handle non-finite values.
Results may differ from a plain program's by a relative error of at most 0.0003.
Values sent between devices are 32-bit elements; how exact they have to be, the bound alone decides.
A program may use at most 64 MiB of HBM per device.

v0:
```python
import jax
import jax.numpy as jnp
from jax import lax
from jax.sharding import PartitionSpec as P

SWEEPS = 6
lowest = 0.05
highest = 2.0
centre = (highest + lowest) / 2.0
half_span = (highest - lowest) / 2.0
bound_ratio = centre / half_span
strength = 4.0


def padded_2(block, sides, width):
    for axis, dim in sides:
        count = lax.axis_size(axis)
        forward = [(i, i + 1) for i in range(count - 1)]
        backward = [(target, source) for source, target in forward]
        low = lax.ppermute(
            lax.slice_in_dim(block, block.shape[dim] - width, None, axis=dim), axis, forward
        )
        high = lax.ppermute(lax.slice_in_dim(block, 0, width, axis=dim), axis, backward)
        block = jnp.concatenate([low, block, high], axis=dim)
    return block


def harmonic(left, right):
    return jnp.where(right > 0, 2.0 * left * right / (left + right), left)


def slope_of(left, right):
    total = left + right
    return jnp.where(right > 0, 2.0 * right * right / (total * total), 1.0)


def neighbours(field, padded):
    widths = [(0, 0)] * (field.ndim - 1) + [(1, 1)]
    deeper = jnp.pad(field, widths)
    return (
        padded[..., :-2, 1:-1, :],
        padded[..., 2:, 1:-1, :],
        padded[..., 1:-1, :-2, :],
        padded[..., 1:-1, 2:, :],
        deeper[..., :-2],
        deeper[..., 2:],
    )


def face_tables(sigma, padded):
    others = neighbours(sigma, padded)
    depth = lax.broadcasted_iota(jnp.int32, sigma.shape, 2)
    surface = depth == 0
    coeffs = [harmonic(sigma, other) for other in others]
    slopes = [slope_of(sigma, other) for other in others]
    coeffs[4] = jnp.where(surface, 0.0, coeffs[4])
    slopes[4] = jnp.where(surface, 0.0, slopes[4])
    return (coeffs, slopes)


def apply_operator(field, padded, coeffs):
    others = neighbours(field, padded)
    total = coeffs[0] * (field - others[0])
    for index in range(1, 6):
        total = total + coeffs[index] * (field - others[index])
    return total


def solve(rhs, start, coeffs, inverse, pad_fn):
    residual = rhs - apply_operator(start, pad_fn(start), coeffs)
    update = inverse * residual / centre
    iterate = start
    factor = 1.0 / bound_ratio
    for sweep in range(SWEEPS):
        iterate = iterate + update
        residual = residual - apply_operator(update, pad_fn(update), coeffs)
        following = 1.0 / (2.0 * bound_ratio - factor)
        update = following * factor * update + 2.0 * following / half_span * (inverse * residual)
        factor = following
    return iterate + update


def gradient_term(potential, adjoint, padded_potential, padded_adjoint, slopes):
    near_potential = neighbours(potential, padded_potential)
    near_adjoint = neighbours(adjoint, padded_adjoint)
    total = slopes[0] * (potential - near_potential[0]) * (adjoint - near_adjoint[0])
    for index in range(1, 6):
        total = total + slopes[index] * (potential - near_potential[index]) * (
            adjoint - near_adjoint[index]
        )
    return total


def pad_joint(field):
    return padded_2(field, (("gx", 1), ("gy", 2)), 1)


def reduce_groups(partial_value, depth):
    summed = lax.psum(partial_value, "src")
    return lax.dynamic_slice_in_dim(summed, lax.axis_index("src") * depth, depth, 2)


def body(warm_potential, warm_adjoint, conductivity, electrodes, receivers, observed, source_order):
    panel = lax.all_gather(conductivity, "src", axis=2, tiled=True)
    group = lax.axis_index("src")
    slots = warm_potential.shape[0]
    width_x = panel.shape[0]
    ny_global = panel.shape[1] * lax.axis_size("gy")
    x_start = lax.axis_index("gx") * width_x
    potential_start, adjoint_start = (warm_potential, warm_adjoint)
    first_slot = group * slots
    y_start = lax.axis_index("gy") * panel.shape[1]
    width_y = panel.shape[1]
    depth_cells = panel.shape[2]
    coeffs, slopes = face_tables(panel, pad_joint(panel[None])[0])
    inverse = 1.0 / (coeffs[0] + coeffs[1] + coeffs[2] + coeffs[3] + coeffs[4] + coeffs[5])
    idents = lax.dynamic_slice_in_dim(source_order, first_slot, slots)
    pairs = jnp.take(electrodes, idents, axis=0)
    rows_observed = jnp.take(observed, idents, axis=0)

    def picker(cells):
        local_x = cells // ny_global - x_start
        local_y = cells % ny_global - y_start
        inside = (local_x >= 0) & (local_x < width_x) & (local_y >= 0) & (local_y < width_y)
        flat = local_x * width_y + local_y
        places = lax.broadcasted_iota(jnp.int32, (cells.shape[0], width_x * width_y), 1)
        return jnp.where((flat[:, None] == places) & inside[:, None], 1.0, 0.0).astype(jnp.float32)

    def on_surface(flat):
        field = jnp.zeros((slots, width_x, width_y, depth_cells), jnp.float32)
        return field.at[..., 0].set(flat.reshape(slots, width_x, width_y))

    source_surface = strength * (picker(pairs[:, 0]) - picker(pairs[:, 1]))
    potential = solve(on_surface(source_surface), potential_start, coeffs, inverse, pad_joint)
    pickup = picker(receivers[:, 0]) - picker(receivers[:, 1])
    top = potential[..., 0].reshape(slots, width_x * width_y)
    local_values = jnp.dot(
        top, pickup.T, precision=lax.Precision.HIGHEST, preferred_element_type=jnp.float32
    )
    predicted = lax.psum(local_values, ("gx", "gy"))
    misfit = predicted - rows_observed
    back = jnp.dot(
        misfit, pickup, precision=lax.Precision.HIGHEST, preferred_element_type=jnp.float32
    )
    adjoint = solve(on_surface(back), adjoint_start, coeffs, inverse, pad_joint)
    padded_both = pad_joint(jnp.concatenate([potential, adjoint], 0))
    term = gradient_term(potential, adjoint, padded_both[:slots], padded_both[slots:], slopes)
    partial_value = -jnp.sum(term, axis=0)
    return reduce_groups(partial_value, conductivity.shape[2])


def solution(mesh):
    in_specs = (
        P("src", "gx", "gy", None),
        P("src", "gx", "gy", None),
        P("gx", "gy", "src"),
        P(),
        P(),
        P(),
        P(),
    )
    out_specs = P("gx", "gy", "src")
    return jax.shard_map(body, mesh=mesh, in_specs=in_specs, out_specs=out_specs, check_vma=False)
```

profile of v0, /device:TPU:16, one launch (start us, length us, event | category | flops | bytes accessed | tf_op | source)
XLA Modules:
  0.0 592.4 jit_solution(16727907163246744626)
XLA Ops:
  7.3 29.0 %all_gather.3 = f32[4,32,128]{1,0,2:T(4,128)S(1)} all-gather(f32[4,32,16]{1,0,2:T(4,128)S(1)} %copy.69), channel_id=1, replica_groups=mesh['src'=8,'gx'=16,'gy'=4] {'src'}, dimensions={2}, use_global_device_ids=true | all-gather | bytes 73728 | tf_op jit(solution)/shard_map/all_gather | solution.py:104
  37.8 3.0 collective-permute-start
  40.9 3.9 collective-permute-start.4
  50.0 5.4 collective-permute-start.3
  55.4 2.6 collective-permute-start.2
  58.0 21.9 %collective-permute-done.3 = f32[1,6,1,128]{2,1,3,0:T(8,128)S(1)} collective-permute-done((f32[1,6,1,128]{2,1,3,0:T(8,128)S(1)}, f32[1,6,1,128]{2,1,3,0:T(8,128)S(1)}, u32[]{:S(2)}, u32[]{:S(2)}) %collective-permute-start.3) | collective-permute-done | bytes 3104 | tf_op jit(solution)/shard_map/ppermute | solution.py:23
  82.3 2.3 collective-permute-start.7
  84.7 5.6 collective-permute-start.6
  90.3 2.0 add_divide_fusion
  96.5 3.0 collective-permute-start.8
  100.5 1.9 collective-permute-start.11
  102.4 6.0 %collective-permute-start.10 = (f32[4,6,1,128]{3,2,1,0:T(1,128)S(1)}, f32[4,6,1,128]{3,2,1,0:T(1,128)S(1)}, u32[]{:S(2)}, u32[]{:S(2)}) collective-permute-start(f32[4,6,1,128]{3,2,1,0:T(1,128)S(1)} %get-tuple-element.118), channel_id=1, source_target_pairs={{0,1},{1,2},{2,3},{4,5},{5,6},{6,7},{8,9},{9,10},{10,11},{12,13},{... | collective-permute-start | bytes 36872 | tf_op jit(solution)/shard_map/ppermute | solution.py:20
  111.4 5.8 collective-permute-start.12
  118.2 1.9 collective-permute-start.15
  120.1 6.0 %collective-permute-start.14 = (f32[4,6,1,128]{3,2,1,0:T(1,128)S(1)}, f32[4,6,1,128]{3,2,1,0:T(1,128)S(1)}, u32[]{:S(2)}, u32[]{:S(2)}) collective-permute-start(f32[4,6,1,128]{3,2,1,0:T(1,128)S(1)} %get-tuple-element.116), channel_id=1, source_target_pairs={{0,1},{1,2},{2,3},{4,5},{5,6},{6,7},{8,9},{9,10},{10,11},{12,13},{... | collective-permute-start | bytes 36872 | tf_op jit(solution)/shard_map/ppermute | solution.py:20
  129.3 5.9 collective-permute-start.16
  136.1 1.9 collective-permute-start.19
  138.0 6.0 %collective-permute-start.18 = (f32[4,6,1,128]{3,2,1,0:T(1,128)S(1)}, f32[4,6,1,128]{3,2,1,0:T(1,128)S(1)}, u32[]{:S(2)}, u32[]{:S(2)}) collective-permute-start(f32[4,6,1,128]{3,2,1,0:T(1,128)S(1)} %get-tuple-element.114), channel_id=1, source_target_pairs={{0,1},{1,2},{2,3},{4,5},{5,6},{6,7},{8,9},{9,10},{10,11},{12,13},{... | collective-permute-start | bytes 36872 | tf_op jit(solution)/shard_map/ppermute | solution.py:20
  144.7 5.5 collective-permute-start.32
  153.2 5.8 collective-permute-start.20
  162.4 6.0 %collective-permute-start.22 = (f32[4,6,1,128]{3,2,1,0:T(1,128)}, f32[4,6,1,128]{3,2,1,0:T(1,128)}, u32[]{:S(2)}, u32[]{:S(2)}) collective-permute-start(f32[4,6,1,128]{3,2,1,0:T(1,128)} %get-tuple-element.112), channel_id=1, source_target_pairs={{0,1},{1,2},{2,3},{4,5},{5,6},{6,7},{8,9},{9,10},{10,11},{12,13},{... | collective-permute-start | bytes 36872 | tf_op jit(solution)/shard_map/ppermute | solution.py:20
  172.6 4.1 collective-permute-start.24
  177.6 1.9 collective-permute-start.27
  179.5 6.0 %collective-permute-start.26 = (f32[4,6,1,128]{3,2,1,0:T(1,128)S(1)}, f32[4,6,1,128]{3,2,1,0:T(1,128)S(1)}, u32[]{:S(2)}, u32[]{:S(2)}) collective-permute-start(f32[4,6,1,128]{3,2,1,0:T(1,128)S(1)} %get-tuple-element.110), channel_id=1, source_target_pairs={{0,1},{1,2},{2,3},{4,5},{5,6},{6,7},{8,9},{9,10},{10,11},{12,13},{... | collective-permute-start | bytes 36872 | tf_op jit(solution)/shard_map/ppermute | solution.py:20
  188.6 5.2 collective-permute-start.28
  196.6 6.0 %collective-permute-start.30 = (f32[4,6,1,128]{3,2,1,0:T(1,128)S(1)}, f32[4,6,1,128]{3,2,1,0:T(1,128)S(1)}, u32[]{:S(2)}, u32[]{:S(2)}) collective-permute-start(f32[4,6,1,128]{3,2,1,0:T(1,128)S(1)} %get-tuple-element.108), channel_id=1, source_target_pairs={{0,1},{1,2},{2,3},{4,5},{5,6},{6,7},{8,9},{9,10},{10,11},{12,13},{... | collective-permute-start | bytes 36872 | tf_op jit(solution)/shard_map/ppermute | solution.py:20
  204.6 6.0 %collective-permute-start.34 = (f32[4,6,1,128]{3,2,1,0:T(1,128)S(1)}, f32[4,6,1,128]{3,2,1,0:T(1,128)S(1)}, u32[]{:S(2)}, u32[]{:S(2)}) collective-permute-start(f32[4,6,1,128]{3,2,1,0:T(1,128)S(1)} %get-tuple-element.106), channel_id=1, source_target_pairs={{0,1},{1,2},{2,3},{4,5},{5,6},{6,7},{8,9},{9,10},{10,11},{12,13},{... | collective-permute-start | bytes 36872 | tf_op jit(solution)/shard_map/ppermute | solution.py:20
  212.4 144.6 %psum.14 = f32[4,128]{1,0:T(4,128)S(1)} all-reduce(f32[4,128]{1,0:T(4,128)S(1)} %fusion.300), channel_id=1, replica_groups=mesh['src'=8,'gx'=16,'gy'=4] {'gx','gy'}, use_global_device_ids=true, to_apply=%region_0.1 | all-reduce | flops 512 | bytes 4096 | tf_op jit(solution)/shard_map/psum | solution.py:140
  359.9 3.0 collective-permute-start.36
  363.9 4.6 collective-permute-start.39
  368.5 3.3 collective-permute-start.38
  371.9 3.1 collective-permute-done.38
  376.6 3.0 collective-permute-start.40
  382.5 6.0 %collective-permute-start.42 = (f32[4,6,1,128]{3,2,1,0:T(1,128)S(1)}, f32[4,6,1,128]{3,2,1,0:T(1,128)S(1)}, u32[]{:S(2)}, u32[]{:S(2)}) collective-permute-start(f32[4,6,1,128]{3,2,1,0:T(1,128)S(1)} %get-tuple-element.102), channel_id=1, source_target_pairs={{0,1},{1,2},{2,3},{4,5},{5,6},{6,7},{8,9},{9,10},{10,11},{12,13},{... | collective-permute-start | bytes 36872 | tf_op jit(solution)/shard_map/ppermute | solution.py:20
  391.5 4.1 collective-permute-start.44
  396.6 1.9 collective-permute-start.47
  398.5 6.2 %collective-permute-start.46 = (f32[4,6,1,128]{3,2,1,0:T(1,128)S(1)}, f32[4,6,1,128]{3,2,1,0:T(1,128)S(1)}, u32[]{:S(2)}, u32[]{:S(2)}) collective-permute-start(f32[4,6,1,128]{3,2,1,0:T(1,128)S(1)} %get-tuple-element.100), channel_id=1, source_target_pairs={{0,1},{1,2},{2,3},{4,5},{5,6},{6,7},{8,9},{9,10},{10,11},{12,13},{... | collective-permute-start | bytes 36872 | tf_op jit(solution)/shard_map/ppermute | solution.py:20
  407.5 5.9 collective-permute-start.48
  414.3 1.9 collective-permute-start.51
  416.3 6.0 %collective-permute-start.50 = (f32[4,6,1,128]{3,2,1,0:T(1,128)S(1)}, f32[4,6,1,128]{3,2,1,0:T(1,128)S(1)}, u32[]{:S(2)}, u32[]{:S(2)}) collective-permute-start(f32[4,6,1,128]{3,2,1,0:T(1,128)S(1)} %get-tuple-element.98), channel_id=1, source_target_pairs={{0,1},{1,2},{2,3},{4,5},{5,6},{6,7},{8,9},{9,10},{10,11},{12,13},{... | collective-permute-start | bytes 36872 | tf_op jit(solution)/shard_map/ppermute | solution.py:20
  425.3 5.6 collective-permute-start.52
  433.7 6.0 %collective-permute-start.54 = (f32[4,6,1,128]{3,2,1,0:T(1,128)S(1)}, f32[4,6,1,128]{3,2,1,0:T(1,128)S(1)}, u32[]{:S(2)}, u32[]{:S(2)}) collective-permute-start(f32[4,6,1,128]{3,2,1,0:T(1,128)S(1)} %get-tuple-element.96), channel_id=1, source_target_pairs={{0,1},{1,2},{2,3},{4,5},{5,6},{6,7},{8,9},{9,10},{10,11},{12,13},{... | collective-permute-start | bytes 36872 | tf_op jit(solution)/shard_map/ppermute | solution.py:20
  442.8 5.6 collective-permute-start.56
  451.2 6.0 %collective-permute-start.58 = (f32[4,6,1,128]{3,2,1,0:T(1,128)S(1)}, f32[4,6,1,128]{3,2,1,0:T(1,128)S(1)}, u32[]{:S(2)}, u32[]{:S(2)}) collective-permute-start(f32[4,6,1,128]{3,2,1,0:T(1,128)S(1)} %get-tuple-element.94), channel_id=1, source_target_pairs={{0,1},{1,2},{2,3},{4,5},{5,6},{6,7},{8,9},{9,10},{10,11},{12,13},{... | collective-permute-start | bytes 36872 | tf_op jit(solution)/shard_map/ppermute | solution.py:20
  460.4 5.7 collective-permute-start.60
  467.2 2.1 collective-permute-start.63
  469.2 6.0 %collective-permute-start.62 = (f32[8,6,1,128]{3,2,1,0:T(1,128)S(1)}, f32[8,6,1,128]{3,2,1,0:T(1,128)S(1)}, u32[]{:S(2)}, u32[]{:S(2)}) collective-permute-start(f32[8,6,1,128]{3,2,1,0:T(1,128)S(1)} %get-tuple-element.82), channel_id=1, source_target_pairs={{0,1},{1,2},{2,3},{4,5},{5,6},{6,7},{8,9},{9,10},{10,11},{12,13},{... | collective-permute-start | bytes 73736 | tf_op jit(solution)/shard_map/ppermute | solution.py:20
  477.8 106.1 %all-reduce.21.cloned.1.call-done = f32[4,32,128]{2,1,0:T(8,128)} async-done(((f32[4,32,128]{2,1,0:T(8,128)}), f32[4,32,128]{2,1,0:T(8,128)}) %all-reduce.21.cloned.1.call-update) | async-done | bytes 65552 | tf_op jit(solution)/shard_map/psum | solution.py:99
  (219 shorter events, 79.5 us)
Async XLA Ops:
  6.5 577.4 %all-reduce.21.cloned.1.call-start = ((), (), s32[]{:S(2)}) async-start(), calls=%async_computation | async-start | bytes 131072 | tf_op jit(solution)/shard_map/psum | solution.py:99
  36.5 13.1 %collective-permute-start.1 = (f32[1,1,32,128]{2,1,3,0:T(1,128)S(1)}, f32[1,1,32,128]{2,1,3,0:T(1,128)S(1)}, u32[]{:S(2)}, u32[]{:S(2)}) collective-permute-start(f32[1,1,32,128]{2,1,3,0:T(1,128)S(1)} %get-tuple-element.153), channel_id=1, source_target_pairs={{4,0},{8,4},{12,8},{16,12},{20,16},{24,20},{28,24},{32,28},{36,32}... | collective-permute-start | bytes 49160 | tf_op jit(solution)/shard_map/ppermute | solution.py:23
  37.8 11.8 %collective-permute-start = (f32[1,1,32,128]{2,1,3,0:T(1,128)S(1)}, f32[1,1,32,128]{2,1,3,0:T(1,128)S(1)}, u32[]{:S(2)}, u32[]{:S(2)}) collective-permute-start(f32[1,1,32,128]{2,1,3,0:T(1,128)S(1)} %get-tuple-element.152), channel_id=1, source_target_pairs={{0,4},{4,8},{8,12},{12,16},{16,20},{20,24},{24,28},{28,32},{32,36}... | collective-permute-start | bytes 49160 | tf_op jit(solution)/shard_map/ppermute | solution.py:20
  40.9 41.4 %collective-permute-start.4 = (f32[4,1,32,128]{3,2,1,0:T(8,128)S(1)}, f32[4,1,32,128]{3,2,1,0:T(8,128)S(1)}, u32[]{:S(2)}, u32[]{:S(2)}) collective-permute-start(f32[4,1,32,128]{3,2,1,0:T(8,128)S(1)} %get-tuple-element.151), channel_id=1, source_target_pairs={{0,4},{4,8},{8,12},{12,16},{16,20},{20,24},{24,28},{28,32},{32,36}... | collective-permute-start | bytes 196616 | tf_op jit(solution)/shard_map/ppermute | solution.py:20
  44.8 37.5 %collective-permute-start.5 = (f32[4,1,32,128]{3,2,1,0:T(8,128)S(1)}, f32[4,1,32,128]{3,2,1,0:T(8,128)S(1)}, u32[]{:S(2)}, u32[]{:S(2)}) collective-permute-start(f32[4,1,32,128]{3,2,1,0:T(8,128)S(1)} %get-tuple-element.150), channel_id=1, source_target_pairs={{4,0},{8,4},{12,8},{16,12},{20,16},{24,20},{28,24},{32,28},{36,32}... | collective-permute-start | bytes 196616 | tf_op jit(solution)/shard_map/ppermute | solution.py:23
  50.0 29.9 %collective-permute-start.3 = (f32[1,6,1,128]{2,1,3,0:T(8,128)S(1)}, f32[1,6,1,128]{2,1,3,0:T(8,128)S(1)}, u32[]{:S(2)}, u32[]{:S(2)}) collective-permute-start(f32[1,6,1,128]{2,1,3,0:T(8,128)S(1)} %get-tuple-element.93), channel_id=1, source_target_pairs={{1,0},{2,1},{3,2},{5,4},{6,5},{7,6},{9,8},{10,9},{11,10},{13,12},{... | collective-permute-start | bytes 9224 | tf_op jit(solution)/shard_map/ppermute | solution.py:23
  55.4 24.5 %collective-permute-start.2 = (f32[1,6,1,128]{2,1,3,0:T(8,128)S(1)}, f32[1,6,1,128]{2,1,3,0:T(8,128)S(1)}, u32[]{:S(2)}, u32[]{:S(2)}) collective-permute-start(f32[1,6,1,128]{2,1,3,0:T(8,128)S(1)} %get-tuple-element.92), channel_id=1, source_target_pairs={{0,1},{1,2},{2,3},{4,5},{5,6},{6,7},{8,9},{9,10},{10,11},{12,13},{... | collective-permute-start | bytes 9224 | tf_op jit(solution)/shard_map/ppermute | solution.py:20
  82.3 11.8 %collective-permute-start.7 = (f32[4,6,1,128]{3,2,1,0:T(1,128)S(1)}, f32[4,6,1,128]{3,2,1,0:T(1,128)S(1)}, u32[]{:S(2)}, u32[]{:S(2)}) collective-permute-start(f32[4,6,1,128]{3,2,1,0:T(1,128)S(1)} %get-tuple-element.121), channel_id=1, source_target_pairs={{1,0},{2,1},{3,2},{5,4},{6,5},{7,6},{9,8},{10,9},{11,10},{13,12},{... | collective-permute-start | bytes 36872 | tf_op jit(solution)/shard_map/ppermute | solution.py:23
  84.7 9.4 %collective-permute-start.6 = (f32[4,6,1,128]{3,2,1,0:T(1,128)S(1)}, f32[4,6,1,128]{3,2,1,0:T(1,128)S(1)}, u32[]{:S(2)}, u32[]{:S(2)}) collective-permute-start(f32[4,6,1,128]{3,2,1,0:T(1,128)S(1)} %get-tuple-element.120), channel_id=1, source_target_pairs={{0,1},{1,2},{2,3},{4,5},{5,6},{6,7},{8,9},{9,10},{10,11},{12,13},{... | collective-permute-start | bytes 36872 | tf_op jit(solution)/shard_map/ppermute | solution.py:20
  100.5 8.0 %collective-permute-start.11 = (f32[4,6,1,128]{3,2,1,0:T(1,128)S(1)}, f32[4,6,1,128]{3,2,1,0:T(1,128)S(1)}, u32[]{:S(2)}, u32[]{:S(2)}) collective-permute-start(f32[4,6,1,128]{3,2,1,0:T(1,128)S(1)} %get-tuple-element.119), channel_id=1, source_target_pairs={{1,0},{2,1},{3,2},{5,4},{6,5},{7,6},{9,8},{10,9},{11,10},{13,12},{... | collective-permute-start | bytes 36872 | tf_op jit(solution)/shard_map/ppermute | solution.py:23
  102.4 7.4 %collective-permute-start.10 = (f32[4,6,1,128]{3,2,1,0:T(1,128)S(1)}, f32[4,6,1,128]{3,2,1,0:T(1,128)S(1)}, u32[]{:S(2)}, u32[]{:S(2)}) collective-permute-start(f32[4,6,1,128]{3,2,1,0:T(1,128)S(1)} %get-tuple-element.118), channel_id=1, source_target_pairs={{0,1},{1,2},{2,3},{4,5},{5,6},{6,7},{8,9},{9,10},{10,11},{12,13},{... | collective-permute-start | bytes 36872 | tf_op jit(solution)/shard_map/ppermute | solution.py:20
  110.1 7.1 %collective-permute-start.13 = (f32[4,1,32,128]{3,2,1,0:T(8,128)S(1)}, f32[4,1,32,128]{3,2,1,0:T(8,128)S(1)}, u32[]{:S(2)}, u32[]{:S(2)}) collective-permute-start(f32[4,1,32,128]{3,2,1,0:T(8,128)S(1)} %get-tuple-element.147), channel_id=1, source_target_pairs={{4,0},{8,4},{12,8},{16,12},{20,16},{24,20},{28,24},{32,28},{36,32}... | collective-permute-start | bytes 196616 | tf_op jit(solution)/shard_map/ppermute | solution.py:23
  118.2 8.0 %collective-permute-start.15 = (f32[4,6,1,128]{3,2,1,0:T(1,128)S(1)}, f32[4,6,1,128]{3,2,1,0:T(1,128)S(1)}, u32[]{:S(2)}, u32[]{:S(2)}) collective-permute-start(f32[4,6,1,128]{3,2,1,0:T(1,128)S(1)} %get-tuple-element.117), channel_id=1, source_target_pairs={{1,0},{2,1},{3,2},{5,4},{6,5},{7,6},{9,8},{10,9},{11,10},{13,12},{... | collective-permute-start | bytes 36872 | tf_op jit(solution)/shard_map/ppermute | solution.py:23
  120.1 7.4 %collective-permute-start.14 = (f32[4,6,1,128]{3,2,1,0:T(1,128)S(1)}, f32[4,6,1,128]{3,2,1,0:T(1,128)S(1)}, u32[]{:S(2)}, u32[]{:S(2)}) collective-permute-start(f32[4,6,1,128]{3,2,1,0:T(1,128)S(1)} %get-tuple-element.116), channel_id=1, source_target_pairs={{0,1},{1,2},{2,3},{4,5},{5,6},{6,7},{8,9},{9,10},{10,11},{12,13},{... | collective-permute-start | bytes 36872 | tf_op jit(solution)/shard_map/ppermute | solution.py:20
  127.8 7.3 %collective-permute-start.17 = (f32[4,1,32,128]{3,2,1,0:T(8,128)S(1)}, f32[4,1,32,128]{3,2,1,0:T(8,128)S(1)}, u32[]{:S(2)}, u32[]{:S(2)}) collective-permute-start(f32[4,1,32,128]{3,2,1,0:T(8,128)S(1)} %get-tuple-element.145), channel_id=1, source_target_pairs={{4,0},{8,4},{12,8},{16,12},{20,16},{24,20},{28,24},{32,28},{36,32}... | collective-permute-start | bytes 196616 | tf_op jit(solution)/shard_map/ppermute | solution.py:23
  129.3 6.8 %collective-permute-start.16 = (f32[4,1,32,128]{3,2,1,0:T(8,128)S(1)}, f32[4,1,32,128]{3,2,1,0:T(8,128)S(1)}, u32[]{:S(2)}, u32[]{:S(2)}) collective-permute-start(f32[4,1,32,128]{3,2,1,0:T(8,128)S(1)} %get-tuple-element.144), channel_id=1, source_target_pairs={{0,4},{4,8},{8,12},{12,16},{16,20},{20,24},{24,28},{28,32},{32,36}... | collective-permute-start | bytes 196616 | tf_op jit(solution)/shard_map/ppermute | solution.py:20
  136.1 15.5 %collective-permute-start.19 = (f32[4,6,1,128]{3,2,1,0:T(1,128)S(1)}, f32[4,6,1,128]{3,2,1,0:T(1,128)S(1)}, u32[]{:S(2)}, u32[]{:S(2)}) collective-permute-start(f32[4,6,1,128]{3,2,1,0:T(1,128)S(1)} %get-tuple-element.115), channel_id=1, source_target_pairs={{1,0},{2,1},{3,2},{5,4},{6,5},{7,6},{9,8},{10,9},{11,10},{13,12},{... | collective-permute-start | bytes 36872 | tf_op jit(solution)/shard_map/ppermute | solution.py:23
  138.0 13.6 %collective-permute-start.18 = (f32[4,6,1,128]{3,2,1,0:T(1,128)S(1)}, f32[4,6,1,128]{3,2,1,0:T(1,128)S(1)}, u32[]{:S(2)}, u32[]{:S(2)}) collective-permute-start(f32[4,6,1,128]{3,2,1,0:T(1,128)S(1)} %get-tuple-element.114), channel_id=1, source_target_pairs={{0,1},{1,2},{2,3},{4,5},{5,6},{6,7},{8,9},{9,10},{10,11},{12,13},{... | collective-permute-start | bytes 36872 | tf_op jit(solution)/shard_map/ppermute | solution.py:20
  144.7 32.0 %collective-permute-start.32 = (f32[4,1,32,128]{3,2,1,0:T(8,128)}, f32[4,1,32,128]{3,2,1,0:T(8,128)S(1)}, u32[]{:S(2)}, u32[]{:S(2)}) collective-permute-start(f32[4,1,32,128]{3,2,1,0:T(8,128)} %get-tuple-element.137), channel_id=1, source_target_pairs={{0,4},{4,8},{8,12},{12,16},{16,20},{20,24},{24,28},{28,32},{32,36}... | collective-permute-start | bytes 196616 | tf_op jit(solution)/shard_map/ppermute | solution.py:20
  150.2 43.6 %collective-permute-start.33 = (f32[4,1,32,128]{3,2,1,0:T(8,128)}, f32[4,1,32,128]{3,2,1,0:T(8,128)}, u32[]{:S(2)}, u32[]{:S(2)}) collective-permute-start(f32[4,1,32,128]{3,2,1,0:T(8,128)} %get-tuple-element.136), channel_id=1, source_target_pairs={{4,0},{8,4},{12,8},{16,12},{20,16},{24,20},{28,24},{32,28},{36,32}... | collective-permute-start | bytes 196616 | tf_op jit(solution)/shard_map/ppermute | solution.py:23
  151.9 7.7 %collective-permute-start.21 = (f32[4,1,32,128]{3,2,1,0:T(8,128)S(1)}, f32[4,1,32,128]{3,2,1,0:T(8,128)S(1)}, u32[]{:S(2)}, u32[]{:S(2)}) collective-permute-start(f32[4,1,32,128]{3,2,1,0:T(8,128)S(1)} %get-tuple-element.143), channel_id=1, source_target_pairs={{4,0},{8,4},{12,8},{16,12},{20,16},{24,20},{28,24},{32,28},{36,32}... | collective-permute-start | bytes 196616 | tf_op jit(solution)/shard_map/ppermute | solution.py:23
  160.5 9.8 %collective-permute-start.23 = (f32[4,6,1,128]{3,2,1,0:T(1,128)}, f32[4,6,1,128]{3,2,1,0:T(1,128)}, u32[]{:S(2)}, u32[]{:S(2)}) collective-permute-start(f32[4,6,1,128]{3,2,1,0:T(1,128)} %get-tuple-element.113), channel_id=1, source_target_pairs={{1,0},{2,1},{3,2},{5,4},{6,5},{7,6},{9,8},{10,9},{11,10},{13,12},{... | collective-permute-start | bytes 36872 | tf_op jit(solution)/shard_map/ppermute | solution.py:23
  162.4 7.8 %collective-permute-start.22 = (f32[4,6,1,128]{3,2,1,0:T(1,128)}, f32[4,6,1,128]{3,2,1,0:T(1,128)}, u32[]{:S(2)}, u32[]{:S(2)}) collective-permute-start(f32[4,6,1,128]{3,2,1,0:T(1,128)} %get-tuple-element.112), channel_id=1, source_target_pairs={{0,1},{1,2},{2,3},{4,5},{5,6},{6,7},{8,9},{9,10},{10,11},{12,13},{... | collective-permute-start | bytes 36872 | tf_op jit(solution)/shard_map/ppermute | solution.py:20
  177.6 8.0 %collective-permute-start.27 = (f32[4,6,1,128]{3,2,1,0:T(1,128)S(1)}, f32[4,6,1,128]{3,2,1,0:T(1,128)S(1)}, u32[]{:S(2)}, u32[]{:S(2)}) collective-permute-start(f32[4,6,1,128]{3,2,1,0:T(1,128)S(1)} %get-tuple-element.111), channel_id=1, source_target_pairs={{1,0},{2,1},{3,2},{5,4},{6,5},{7,6},{9,8},{10,9},{11,10},{13,12},{... | collective-permute-start | bytes 36872 | tf_op jit(solution)/shard_map/ppermute | solution.py:23
  179.5 7.4 %collective-permute-start.26 = (f32[4,6,1,128]{3,2,1,0:T(1,128)S(1)}, f32[4,6,1,128]{3,2,1,0:T(1,128)S(1)}, u32[]{:S(2)}, u32[]{:S(2)}) collective-permute-start(f32[4,6,1,128]{3,2,1,0:T(1,128)S(1)} %get-tuple-element.110), channel_id=1, source_target_pairs={{0,1},{1,2},{2,3},{4,5},{5,6},{6,7},{8,9},{9,10},{10,11},{12,13},{... | collective-permute-start | bytes 36872 | tf_op jit(solution)/shard_map/ppermute | solution.py:20
  187.3 7.4 %collective-permute-start.29 = (f32[4,1,32,128]{3,2,1,0:T(8,128)S(1)}, f32[4,1,32,128]{3,2,1,0:T(8,128)S(1)}, u32[]{:S(2)}, u32[]{:S(2)}) collective-permute-start(f32[4,1,32,128]{3,2,1,0:T(8,128)S(1)} %get-tuple-element.139), channel_id=1, source_target_pairs={{4,0},{8,4},{12,8},{16,12},{20,16},{24,20},{28,24},{32,28},{36,32}... | collective-permute-start | bytes 196616 | tf_op jit(solution)/shard_map/ppermute | solution.py:23
  194.7 16.0 %collective-permute-start.31 = (f32[4,6,1,128]{3,2,1,0:T(1,128)S(1)}, f32[4,6,1,128]{3,2,1,0:T(1,128)S(1)}, u32[]{:S(2)}, u32[]{:S(2)}) collective-permute-start(f32[4,6,1,128]{3,2,1,0:T(1,128)S(1)} %get-tuple-element.109), channel_id=1, source_target_pairs={{1,0},{2,1},{3,2},{5,4},{6,5},{7,6},{9,8},{10,9},{11,10},{13,12},{... | collective-permute-start | bytes 36872 | tf_op jit(solution)/shard_map/ppermute | solution.py:23
  196.6 14.0 %collective-permute-start.30 = (f32[4,6,1,128]{3,2,1,0:T(1,128)S(1)}, f32[4,6,1,128]{3,2,1,0:T(1,128)S(1)}, u32[]{:S(2)}, u32[]{:S(2)}) collective-permute-start(f32[4,6,1,128]{3,2,1,0:T(1,128)S(1)} %get-tuple-element.108), channel_id=1, source_target_pairs={{0,1},{1,2},{2,3},{4,5},{5,6},{6,7},{8,9},{9,10},{10,11},{12,13},{... | collective-permute-start | bytes 36872 | tf_op jit(solution)/shard_map/ppermute | solution.py:20
  202.7 154.8 %collective-permute-start.35 = (f32[4,6,1,128]{3,2,1,0:T(1,128)S(1)}, f32[4,6,1,128]{3,2,1,0:T(1,128)S(1)}, u32[]{:S(2)}, u32[]{:S(2)}) collective-permute-start(f32[4,6,1,128]{3,2,1,0:T(1,128)S(1)} %get-tuple-element.107), channel_id=1, source_target_pairs={{1,0},{2,1},{3,2},{5,4},{6,5},{7,6},{9,8},{10,9},{11,10},{13,12},{... | collective-permute-start | bytes 36872 | tf_op jit(solution)/shard_map/ppermute | solution.py:23
  204.6 152.9 %collective-permute-start.34 = (f32[4,6,1,128]{3,2,1,0:T(1,128)S(1)}, f32[4,6,1,128]{3,2,1,0:T(1,128)S(1)}, u32[]{:S(2)}, u32[]{:S(2)}) collective-permute-start(f32[4,6,1,128]{3,2,1,0:T(1,128)S(1)} %get-tuple-element.106), channel_id=1, source_target_pairs={{0,1},{1,2},{2,3},{4,5},{5,6},{6,7},{8,9},{9,10},{10,11},{12,13},{... | collective-permute-start | bytes 36872 | tf_op jit(solution)/shard_map/ppermute | solution.py:20
  363.9 8.0 %collective-permute-start.39 = (f32[4,6,1,128]{3,2,1,0:T(1,128)S(1)}, f32[4,6,1,128]{3,2,1,0:T(1,128)S(1)}, u32[]{:S(2)}, u32[]{:S(2)}) collective-permute-start(f32[4,6,1,128]{3,2,1,0:T(1,128)S(1)} %get-tuple-element.105), channel_id=1, source_target_pairs={{1,0},{2,1},{3,2},{5,4},{6,5},{7,6},{9,8},{10,9},{11,10},{13,12},{... | collective-permute-start | bytes 36872 | tf_op jit(solution)/shard_map/ppermute | solution.py:23
  380.6 8.0 %collective-permute-start.43 = (f32[4,6,1,128]{3,2,1,0:T(1,128)S(1)}, f32[4,6,1,128]{3,2,1,0:T(1,128)S(1)}, u32[]{:S(2)}, u32[]{:S(2)}) collective-permute-start(f32[4,6,1,128]{3,2,1,0:T(1,128)S(1)} %get-tuple-element.103), channel_id=1, source_target_pairs={{1,0},{2,1},{3,2},{5,4},{6,5},{7,6},{9,8},{10,9},{11,10},{13,12},{... | collective-permute-start | bytes 36872 | tf_op jit(solution)/shard_map/ppermute | solution.py:23
  382.5 7.4 %collective-permute-start.42 = (f32[4,6,1,128]{3,2,1,0:T(1,128)S(1)}, f32[4,6,1,128]{3,2,1,0:T(1,128)S(1)}, u32[]{:S(2)}, u32[]{:S(2)}) collective-permute-start(f32[4,6,1,128]{3,2,1,0:T(1,128)S(1)} %get-tuple-element.102), channel_id=1, source_target_pairs={{0,1},{1,2},{2,3},{4,5},{5,6},{6,7},{8,9},{9,10},{10,11},{12,13},{... | collective-permute-start | bytes 36872 | tf_op jit(solution)/shard_map/ppermute | solution.py:20
  396.6 8.2 %collective-permute-start.47 = (f32[4,6,1,128]{3,2,1,0:T(1,128)S(1)}, f32[4,6,1,128]{3,2,1,0:T(1,128)S(1)}, u32[]{:S(2)}, u32[]{:S(2)}) collective-permute-start(f32[4,6,1,128]{3,2,1,0:T(1,128)S(1)} %get-tuple-element.101), channel_id=1, source_target_pairs={{1,0},{2,1},{3,2},{5,4},{6,5},{7,6},{9,8},{10,9},{11,10},{13,12},{... | collective-permute-start | bytes 36872 | tf_op jit(solution)/shard_map/ppermute | solution.py:23
  398.5 7.4 %collective-permute-start.46 = (f32[4,6,1,128]{3,2,1,0:T(1,128)S(1)}, f32[4,6,1,128]{3,2,1,0:T(1,128)S(1)}, u32[]{:S(2)}, u32[]{:S(2)}) collective-permute-start(f32[4,6,1,128]{3,2,1,0:T(1,128)S(1)} %get-tuple-element.100), channel_id=1, source_target_pairs={{0,1},{1,2},{2,3},{4,5},{5,6},{6,7},{8,9},{9,10},{10,11},{12,13},{... | collective-permute-start | bytes 36872 | tf_op jit(solution)/shard_map/ppermute | solution.py:20
  406.2 7.2 %collective-permute-start.49 = (f32[4,1,32,128]{3,2,1,0:T(8,128)S(1)}, f32[4,1,32,128]{3,2,1,0:T(8,128)S(1)}, u32[]{:S(2)}, u32[]{:S(2)}) collective-permute-start(f32[4,1,32,128]{3,2,1,0:T(8,128)S(1)} %get-tuple-element.129), channel_id=1, source_target_pairs={{4,0},{8,4},{12,8},{16,12},{20,16},{24,20},{28,24},{32,28},{36,32}... | collective-permute-start | bytes 196616 | tf_op jit(solution)/shard_map/ppermute | solution.py:23
  407.5 6.8 %collective-permute-start.48 = (f32[4,1,32,128]{3,2,1,0:T(8,128)S(1)}, f32[4,1,32,128]{3,2,1,0:T(8,128)S(1)}, u32[]{:S(2)}, u32[]{:S(2)}) collective-permute-start(f32[4,1,32,128]{3,2,1,0:T(8,128)S(1)} %get-tuple-element.128), channel_id=1, source_target_pairs={{0,4},{4,8},{8,12},{12,16},{16,20},{20,24},{24,28},{28,32},{32,36}... | collective-permute-start | bytes 196616 | tf_op jit(solution)/shard_map/ppermute | solution.py:20
  414.3 8.0 %collective-permute-start.51 = (f32[4,6,1,128]{3,2,1,0:T(1,128)S(1)}, f32[4,6,1,128]{3,2,1,0:T(1,128)S(1)}, u32[]{:S(2)}, u32[]{:S(2)}) collective-permute-start(f32[4,6,1,128]{3,2,1,0:T(1,128)S(1)} %get-tuple-element.99), channel_id=1, source_target_pairs={{1,0},{2,1},{3,2},{5,4},{6,5},{7,6},{9,8},{10,9},{11,10},{13,12},{... | collective-permute-start | bytes 36872 | tf_op jit(solution)/shard_map/ppermute | solution.py:23
  416.3 7.4 %collective-permute-start.50 = (f32[4,6,1,128]{3,2,1,0:T(1,128)S(1)}, f32[4,6,1,128]{3,2,1,0:T(1,128)S(1)}, u32[]{:S(2)}, u32[]{:S(2)}) collective-permute-start(f32[4,6,1,128]{3,2,1,0:T(1,128)S(1)} %get-tuple-element.98), channel_id=1, source_target_pairs={{0,1},{1,2},{2,3},{4,5},{5,6},{6,7},{8,9},{9,10},{10,11},{12,13},{... | collective-permute-start | bytes 36872 | tf_op jit(solution)/shard_map/ppermute | solution.py:20
  424.0 6.9 %collective-permute-start.53 = (f32[4,1,32,128]{3,2,1,0:T(8,128)S(1)}, f32[4,1,32,128]{3,2,1,0:T(8,128)S(1)}, u32[]{:S(2)}, u32[]{:S(2)}) collective-permute-start(f32[4,1,32,128]{3,2,1,0:T(8,128)S(1)} %get-tuple-element.127), channel_id=1, source_target_pairs={{4,0},{8,4},{12,8},{16,12},{20,16},{24,20},{28,24},{32,28},{36,32}... | collective-permute-start | bytes 196616 | tf_op jit(solution)/shard_map/ppermute | solution.py:23
  431.8 8.0 %collective-permute-start.55 = (f32[4,6,1,128]{3,2,1,0:T(1,128)S(1)}, f32[4,6,1,128]{3,2,1,0:T(1,128)S(1)}, u32[]{:S(2)}, u32[]{:S(2)}) collective-permute-start(f32[4,6,1,128]{3,2,1,0:T(1,128)S(1)} %get-tuple-element.97), channel_id=1, source_target_pairs={{1,0},{2,1},{3,2},{5,4},{6,5},{7,6},{9,8},{10,9},{11,10},{13,12},{... | collective-permute-start | bytes 36872 | tf_op jit(solution)/shard_map/ppermute | solution.py:23
  433.7 7.4 %collective-permute-start.54 = (f32[4,6,1,128]{3,2,1,0:T(1,128)S(1)}, f32[4,6,1,128]{3,2,1,0:T(1,128)S(1)}, u32[]{:S(2)}, u32[]{:S(2)}) collective-permute-start(f32[4,6,1,128]{3,2,1,0:T(1,128)S(1)} %get-tuple-element.96), channel_id=1, source_target_pairs={{0,1},{1,2},{2,3},{4,5},{5,6},{6,7},{8,9},{9,10},{10,11},{12,13},{... | collective-permute-start | bytes 36872 | tf_op jit(solution)/shard_map/ppermute | solution.py:20
  441.5 6.9 %collective-permute-start.57 = (f32[4,1,32,128]{3,2,1,0:T(8,128)S(1)}, f32[4,1,32,128]{3,2,1,0:T(8,128)S(1)}, u32[]{:S(2)}, u32[]{:S(2)}) collective-permute-start(f32[4,1,32,128]{3,2,1,0:T(8,128)S(1)} %get-tuple-element.125), channel_id=1, source_target_pairs={{4,0},{8,4},{12,8},{16,12},{20,16},{24,20},{28,24},{32,28},{36,32}... | collective-permute-start | bytes 196616 | tf_op jit(solution)/shard_map/ppermute | solution.py:23
  449.3 8.0 %collective-permute-start.59 = (f32[4,6,1,128]{3,2,1,0:T(1,128)S(1)}, f32[4,6,1,128]{3,2,1,0:T(1,128)S(1)}, u32[]{:S(2)}, u32[]{:S(2)}) collective-permute-start(f32[4,6,1,128]{3,2,1,0:T(1,128)S(1)} %get-tuple-element.95), channel_id=1, source_target_pairs={{1,0},{2,1},{3,2},{5,4},{6,5},{7,6},{9,8},{10,9},{11,10},{13,12},{... | collective-permute-start | bytes 36872 | tf_op jit(solution)/shard_map/ppermute | solution.py:23
  451.2 7.4 %collective-permute-start.58 = (f32[4,6,1,128]{3,2,1,0:T(1,128)S(1)}, f32[4,6,1,128]{3,2,1,0:T(1,128)S(1)}, u32[]{:S(2)}, u32[]{:S(2)}) collective-permute-start(f32[4,6,1,128]{3,2,1,0:T(1,128)S(1)} %get-tuple-element.94), channel_id=1, source_target_pairs={{0,1},{1,2},{2,3},{4,5},{5,6},{6,7},{8,9},{9,10},{10,11},{12,13},{... | collective-permute-start | bytes 36872 | tf_op jit(solution)/shard_map/ppermute | solution.py:20
  459.1 7.1 %collective-permute-start.61 = (f32[8,1,32,128]{3,2,1,0:T(8,128)S(1)}, f32[8,1,32,128]{3,2,1,0:T(8,128)S(1)}, u32[]{:S(2)}, u32[]{:S(2)}) collective-permute-start(f32[8,1,32,128]{3,2,1,0:T(8,128)S(1)} %get-tuple-element.91), channel_id=1, source_target_pairs={{4,0},{8,4},{12,8},{16,12},{20,16},{24,20},{28,24},{32,28},{36,32}... | collective-permute-start | bytes 393224 | tf_op jit(solution)/shard_map/ppermute | solution.py:23
  467.2 8.8 %collective-permute-start.63 = (f32[8,6,1,128]{3,2,1,0:T(1,128)S(1)}, f32[8,6,1,128]{3,2,1,0:T(1,128)S(1)}, u32[]{:S(2)}, u32[]{:S(2)}) collective-permute-start(f32[8,6,1,128]{3,2,1,0:T(1,128)S(1)} %get-tuple-element.83), channel_id=1, source_target_pairs={{1,0},{2,1},{3,2},{5,4},{6,5},{7,6},{9,8},{10,9},{11,10},{13,12},{... | collective-permute-start | bytes 73736 | tf_op jit(solution)/shard_map/ppermute | solution.py:23
  469.2 7.5 %collective-permute-start.62 = (f32[8,6,1,128]{3,2,1,0:T(1,128)S(1)}, f32[8,6,1,128]{3,2,1,0:T(1,128)S(1)}, u32[]{:S(2)}, u32[]{:S(2)}) collective-permute-start(f32[8,6,1,128]{3,2,1,0:T(1,128)S(1)} %get-tuple-element.82), channel_id=1, source_target_pairs={{0,1},{1,2},{2,3},{4,5},{5,6},{6,7},{8,9},{9,10},{10,11},{12,13},{... | collective-permute-start | bytes 73736 | tf_op jit(solution)/shard_map/ppermute | solution.py:20
  (38 other events, 802.2 us)
Sparse Core Ops, SparseCore 0:
  477.9 105.9 all-reduce.20
where the time goes:
time: 595 us; the launch traced here: 592 us
  starting transfers between devices  224 us (38%)
  blocking collectives  174 us (29%)
  waiting for transfers between devices  153 us (26%)
  other arithmetic  15 us (3%)
  between operations  14.6 us (2%)
  local copies, waits for them, and re-layouts  12.1 us (2%)
    ppermute x32, starting transfers between devices, padded_2(): lax.ppermute(lax.slice_in_dim(block, block.shape[dim] - width, None, axis...  166 us
    psum x1, blocking collectives, body(): predicted = lax.psum(local_values, ('gx', 'gy'))  145 us
    psum x1, waiting for transfers between devices, reduce_groups(): summed = lax.psum(partial_value, 'src')  106 us
    ppermute x32, starting transfers between devices, padded_2(): lax.ppermute(lax.slice_in_dim(block, 0, width, axis=dim), axis, backward)  58.2 us
    all_gather x1, blocking collectives, body(): panel = lax.all_gather(conductivity, 'src', axis=2, tiled=True)  29 us
    ppermute x32, waiting for transfers between devices, padded_2(): lax.ppermute(lax.slice_in_dim(block, block.shape[dim] - width, None, axis...  24.7 us
    ppermute x32, waiting for transfers between devices, padded_2(): lax.ppermute(lax.slice_in_dim(block, 0, width, axis=dim), axis, backward)  22 us
  transfers between devices with their start and end apart: 65, of which 24 were waited for; matrix products, arithmetic and copies ran while one was open for 3% of the time, Pallas kernels for 0%

commit v1 on v0

--- a/solution.py
+++ b/solution.py
@@ -96,7 +96,7 @@
 
 
 def reduce_groups(partial_value, depth):
-    summed = lax.psum(partial_value, "src")
+    summed = jnp.sum(lax.all_gather(partial_value, "src"), axis=0)
     return lax.dynamic_slice_in_dim(summed, lax.axis_index("src") * depth, depth, 2)
 
 

time: 595 us -> 526 us (0.88)
  the two profiles are of different devices: /device:TPU:16 before, /device:TPU:304 now
where the time goes in v1:
time: 526 us; the launch traced here: 524 us
  blocking collectives  197 us (37%)
  starting transfers between devices  162 us (31%)
  waiting for transfers between devices  138 us (26%)
  other arithmetic  14.4 us (3%)
  local copies, waits for them, and re-layouts  10.5 us (2%)
    psum x1, blocking collectives, body(): predicted = lax.psum(local_values, ('gx', 'gy'))  138 us
    ppermute x32, waiting for transfers between devices, padded_2(): lax.ppermute(lax.slice_in_dim(block, block.shape[dim] - width, None, axis...  118 us
    ppermute x32, starting transfers between devices, padded_2(): lax.ppermute(lax.slice_in_dim(block, 0, width, axis=dim), axis, backward)  103 us
    ppermute x32, starting transfers between devices, padded_2(): lax.ppermute(lax.slice_in_dim(block, block.shape[dim] - width, None, axis...  59.1 us
    all_gather x1, blocking collectives, reduce_groups(): summed = jnp.sum(lax.all_gather(partial_value, 'src'), axis=0)  30.1 us
    all_gather x1, blocking collectives, body(): panel = lax.all_gather(conductivity, 'src', axis=2, tiled=True)  29 us
    ppermute x32, waiting for transfers between devices, padded_2(): lax.ppermute(lax.slice_in_dim(block, 0, width, axis=dim), axis, backward)  20.6 us
  transfers between devices with their start and end apart: 64, of which 35 were waited for; matrix products, arithmetic and copies ran while one was open for 3% of the time, Pallas kernels for 0%

profile of v1, /device:TPU:304, one launch (start us, length us, event | category | flops | bytes accessed | tf_op | source)
XLA Modules:
  0.0 524.3 jit_solution(12182399868592908232)
XLA Ops:
  0.8 29.0 %all_gather.7 = f32[4,32,128]{1,0,2:T(4,128)S(1)} all-gather(f32[4,32,16]{1,0,2:T(4,128)S(1)} %copy.68), channel_id=1, replica_groups=mesh['src'=8,'gx'=16,'gy'=4] {'src'}, dimensions={2}, use_global_device_ids=true | all-gather | bytes 73728 | tf_op jit(solution)/shard_map/all_gather | solution.py:104
  37.3 3.8 collective-permute-start.5
  45.0 4.1 collective-permute-start.3
  50.4 19.9 %collective-permute-done.3 = f32[1,6,1,128]{2,1,3,0:T(8,128)S(1)} collective-permute-done((f32[1,6,1,128]{2,1,3,0:T(8,128)S(1)}, f32[1,6,1,128]{2,1,3,0:T(8,128)S(1)}, u32[]{:S(2)}, u32[]{:S(2)}) %collective-permute-start.3) | collective-permute-done | bytes 3104 | tf_op jit(solution)/shard_map/ppermute | solution.py:23
  70.3 5.1 collective-permute-done.2
  77.8 3.5 collective-permute-start.7
  92.4 4.4 collective-permute-done.8
  96.8 5.0 collective-permute-start.11
  103.2 5.1 collective-permute-done.10
  113.0 4.4 collective-permute-done.12
  117.4 4.6 collective-permute-start.15
  123.4 5.1 collective-permute-done.14
  133.3 4.4 collective-permute-done.16
  137.7 3.1 collective-permute-start.19
  144.7 4.9 collective-permute-start.33
  154.8 3.8 collective-permute-done.20
  159.2 6.0 %collective-permute-start.23 = (f32[4,6,1,128]{3,2,1,0:T(1,128)}, f32[4,6,1,128]{3,2,1,0:T(1,128)}, u32[]{:S(2)}, u32[]{:S(2)}) collective-permute-start(f32[4,6,1,128]{3,2,1,0:T(1,128)} %get-tuple-element.113), channel_id=1, source_target_pairs={{1,0},{2,1},{3,2},{5,4},{6,5},{7,6},{9,8},{10,9},{11,10},{13,12},{... | collective-permute-start | bytes 36872 | tf_op jit(solution)/shard_map/ppermute | solution.py:23
  168.4 3.7 collective-permute-done.22
  177.4 4.3 collective-permute-done.24
  181.8 3.8 collective-permute-start.27
  187.0 5.1 collective-permute-done.26
  197.6 3.5 collective-permute-done.28
  201.1 3.1 collective-permute-start.31
  205.6 5.4 %collective-permute-start.35 = (f32[4,6,1,128]{3,2,1,0:T(1,128)S(1)}, f32[4,6,1,128]{3,2,1,0:T(1,128)S(1)}, u32[]{:S(2)}, u32[]{:S(2)}) collective-permute-start(f32[4,6,1,128]{3,2,1,0:T(1,128)S(1)} %get-tuple-element.107), channel_id=1, source_target_pairs={{1,0},{2,1},{3,2},{5,4},{6,5},{7,6},{9,8},{10,9},{11,10},{13,12},{... | collective-permute-start | bytes 36872 | tf_op jit(solution)/shard_map/ppermute | solution.py:23
  214.0 138.3 %psum.7 = f32[4,128]{1,0:T(4,128)S(1)} all-reduce(f32[4,128]{1,0:T(4,128)S(1)} %fusion.300), channel_id=1, replica_groups=mesh['src'=8,'gx'=16,'gy'=4] {'gx','gy'}, use_global_device_ids=true, to_apply=%region_0.1 | all-reduce | flops 512 | bytes 4096 | tf_op jit(solution)/shard_map/psum | solution.py:140
  354.1 3.9 collective-permute-start.37
  359.9 4.9 collective-permute-done.36
  364.8 3.6 collective-permute-start.39
  369.8 5.1 collective-permute-done.38
  379.5 4.4 collective-permute-done.40
  383.9 4.8 collective-permute-start.43
  390.2 5.1 collective-permute-done.42
  399.9 4.4 collective-permute-done.44
  404.3 5.6 %collective-permute-start.47 = (f32[4,6,1,128]{3,2,1,0:T(1,128)S(1)}, f32[4,6,1,128]{3,2,1,0:T(1,128)S(1)}, u32[]{:S(2)}, u32[]{:S(2)}) collective-permute-start(f32[4,6,1,128]{3,2,1,0:T(1,128)S(1)} %get-tuple-element.101), channel_id=1, source_target_pairs={{1,0},{2,1},{3,2},{5,4},{6,5},{7,6},{9,8},{10,9},{11,10},{13,12},{... | collective-permute-start | bytes 36872 | tf_op jit(solution)/shard_map/ppermute | solution.py:23
  411.4 5.0 collective-permute-done.46
  421.1 4.4 collective-permute-done.48
  425.4 3.1 collective-permute-start.51
  430.0 5.1 collective-permute-done.50
  439.7 4.4 collective-permute-done.52
  444.1 3.1 collective-permute-start.55
  448.7 5.1 collective-permute-done.54
  458.4 4.4 collective-permute-done.56
  462.8 3.1 collective-permute-start.59
  467.4 5.1 collective-permute-done.58
  477.4 5.1 collective-permute-done.60
  482.5 3.3 collective-permute-start.63
  487.8 5.1 collective-permute-done.62
  493.4 30.1 %all-gather = f32[32,32,128]{2,1,0:T(8,128)S(1)} all-gather(f32[4,32,128]{2,1,0:T(8,128)S(1)} %neg.13), channel_id=2, replica_groups=mesh['src'=8,'gx'=16,'gy'=4] {'src'}, dimensions={0}, use_global_device_ids=true | all-gather | bytes 589824 | tf_op jit(solution)/shard_map/all_gather | solution.py:99
  (218 shorter events, 111.7 us)
Async XLA Ops:
  29.9 14.7 %collective-permute-start.1 = (f32[1,1,32,128]{2,1,3,0:T(1,128)S(1)}, f32[1,1,32,128]{2,1,3,0:T(1,128)S(1)}, u32[]{:S(2)}, u32[]{:S(2)}) collective-permute-start(f32[1,1,32,128]{2,1,3,0:T(1,128)S(1)} %get-tuple-element.153), channel_id=1, source_target_pairs={{4,0},{8,4},{12,8},{16,12},{20,16},{24,20},{28,24},{32,28},{36,32}... | collective-permute-start | bytes 49160 | tf_op jit(solution)/shard_map/ppermute | solution.py:23
  31.9 12.7 %collective-permute-start = (f32[1,1,32,128]{2,1,3,0:T(1,128)S(1)}, f32[1,1,32,128]{2,1,3,0:T(1,128)S(1)}, u32[]{:S(2)}, u32[]{:S(2)}) collective-permute-start(f32[1,1,32,128]{2,1,3,0:T(1,128)S(1)} %get-tuple-element.152), channel_id=1, source_target_pairs={{0,4},{4,8},{8,12},{12,16},{16,20},{20,24},{24,28},{28,32},{32,36}... | collective-permute-start | bytes 49160 | tf_op jit(solution)/shard_map/ppermute | solution.py:20
  34.3 43.4 %collective-permute-start.4 = (f32[4,1,32,128]{3,2,1,0:T(8,128)S(1)}, f32[4,1,32,128]{3,2,1,0:T(8,128)S(1)}, u32[]{:S(2)}, u32[]{:S(2)}) collective-permute-start(f32[4,1,32,128]{3,2,1,0:T(8,128)S(1)} %get-tuple-element.151), channel_id=1, source_target_pairs={{0,4},{4,8},{8,12},{12,16},{16,20},{20,24},{24,28},{28,32},{32,36}... | collective-permute-start | bytes 196616 | tf_op jit(solution)/shard_map/ppermute | solution.py:20
  37.3 40.4 %collective-permute-start.5 = (f32[4,1,32,128]{3,2,1,0:T(8,128)S(1)}, f32[4,1,32,128]{3,2,1,0:T(8,128)S(1)}, u32[]{:S(2)}, u32[]{:S(2)}) collective-permute-start(f32[4,1,32,128]{3,2,1,0:T(8,128)S(1)} %get-tuple-element.150), channel_id=1, source_target_pairs={{4,0},{8,4},{12,8},{16,12},{20,16},{24,20},{28,24},{32,28},{36,32}... | collective-permute-start | bytes 196616 | tf_op jit(solution)/shard_map/ppermute | solution.py:23
  45.0 25.3 %collective-permute-start.3 = (f32[1,6,1,128]{2,1,3,0:T(8,128)S(1)}, f32[1,6,1,128]{2,1,3,0:T(8,128)S(1)}, u32[]{:S(2)}, u32[]{:S(2)}) collective-permute-start(f32[1,6,1,128]{2,1,3,0:T(8,128)S(1)} %get-tuple-element.93), channel_id=1, source_target_pairs={{1,0},{2,1},{3,2},{5,4},{6,5},{7,6},{9,8},{10,9},{11,10},{13,12},{... | collective-permute-start | bytes 9224 | tf_op jit(solution)/shard_map/ppermute | solution.py:23
  49.1 26.3 %collective-permute-start.2 = (f32[1,6,1,128]{2,1,3,0:T(8,128)S(1)}, f32[1,6,1,128]{2,1,3,0:T(8,128)S(1)}, u32[]{:S(2)}, u32[]{:S(2)}) collective-permute-start(f32[1,6,1,128]{2,1,3,0:T(8,128)S(1)} %get-tuple-element.92), channel_id=1, source_target_pairs={{0,1},{1,2},{2,3},{4,5},{5,6},{6,7},{8,9},{9,10},{10,11},{12,13},{... | collective-permute-start | bytes 9224 | tf_op jit(solution)/shard_map/ppermute | solution.py:20
  77.8 8.6 %collective-permute-start.7 = (f32[4,6,1,128]{3,2,1,0:T(1,128)S(1)}, f32[4,6,1,128]{3,2,1,0:T(1,128)S(1)}, u32[]{:S(2)}, u32[]{:S(2)}) collective-permute-start(f32[4,6,1,128]{3,2,1,0:T(1,128)S(1)} %get-tuple-element.121), channel_id=1, source_target_pairs={{1,0},{2,1},{3,2},{5,4},{6,5},{7,6},{9,8},{10,9},{11,10},{13,12},{... | collective-permute-start | bytes 36872 | tf_op jit(solution)/shard_map/ppermute | solution.py:23
  81.3 6.5 %collective-permute-start.6 = (f32[4,6,1,128]{3,2,1,0:T(1,128)S(1)}, f32[4,6,1,128]{3,2,1,0:T(1,128)S(1)}, u32[]{:S(2)}, u32[]{:S(2)}) collective-permute-start(f32[4,6,1,128]{3,2,1,0:T(1,128)S(1)} %get-tuple-element.120), channel_id=1, source_target_pairs={{0,1},{1,2},{2,3},{4,5},{5,6},{6,7},{8,9},{9,10},{10,11},{12,13},{... | collective-permute-start | bytes 36872 | tf_op jit(solution)/shard_map/ppermute | solution.py:20
  90.0 6.8 %collective-permute-start.8 = (f32[4,1,32,128]{3,2,1,0:T(8,128)S(1)}, f32[4,1,32,128]{3,2,1,0:T(8,128)S(1)}, u32[]{:S(2)}, u32[]{:S(2)}) collective-permute-start(f32[4,1,32,128]{3,2,1,0:T(8,128)S(1)} %get-tuple-element.148), channel_id=1, source_target_pairs={{0,4},{4,8},{8,12},{12,16},{16,20},{20,24},{24,28},{28,32},{32,36}... | collective-permute-start | bytes 196616 | tf_op jit(solution)/shard_map/ppermute | solution.py:20
  96.8 6.4 %collective-permute-start.11 = (f32[4,6,1,128]{3,2,1,0:T(1,128)S(1)}, f32[4,6,1,128]{3,2,1,0:T(1,128)S(1)}, u32[]{:S(2)}, u32[]{:S(2)}) collective-permute-start(f32[4,6,1,128]{3,2,1,0:T(1,128)S(1)} %get-tuple-element.119), channel_id=1, source_target_pairs={{1,0},{2,1},{3,2},{5,4},{6,5},{7,6},{9,8},{10,9},{11,10},{13,12},{... | collective-permute-start | bytes 36872 | tf_op jit(solution)/shard_map/ppermute | solution.py:23
  101.8 6.5 %collective-permute-start.10 = (f32[4,6,1,128]{3,2,1,0:T(1,128)S(1)}, f32[4,6,1,128]{3,2,1,0:T(1,128)S(1)}, u32[]{:S(2)}, u32[]{:S(2)}) collective-permute-start(f32[4,6,1,128]{3,2,1,0:T(1,128)S(1)} %get-tuple-element.118), channel_id=1, source_target_pairs={{0,1},{1,2},{2,3},{4,5},{5,6},{6,7},{8,9},{9,10},{10,11},{12,13},{... | collective-permute-start | bytes 36872 | tf_op jit(solution)/shard_map/ppermute | solution.py:20
  110.5 6.8 %collective-permute-start.12 = (f32[4,1,32,128]{3,2,1,0:T(8,128)S(1)}, f32[4,1,32,128]{3,2,1,0:T(8,128)S(1)}, u32[]{:S(2)}, u32[]{:S(2)}) collective-permute-start(f32[4,1,32,128]{3,2,1,0:T(8,128)S(1)} %get-tuple-element.146), channel_id=1, source_target_pairs={{0,4},{4,8},{8,12},{12,16},{16,20},{20,24},{24,28},{28,32},{32,36}... | collective-permute-start | bytes 196616 | tf_op jit(solution)/shard_map/ppermute | solution.py:20
  117.4 6.0 %collective-permute-start.15 = (f32[4,6,1,128]{3,2,1,0:T(1,128)S(1)}, f32[4,6,1,128]{3,2,1,0:T(1,128)S(1)}, u32[]{:S(2)}, u32[]{:S(2)}) collective-permute-start(f32[4,6,1,128]{3,2,1,0:T(1,128)S(1)} %get-tuple-element.117), channel_id=1, source_target_pairs={{1,0},{2,1},{3,2},{5,4},{6,5},{7,6},{9,8},{10,9},{11,10},{13,12},{... | collective-permute-start | bytes 36872 | tf_op jit(solution)/shard_map/ppermute | solution.py:23
  122.0 6.5 %collective-permute-start.14 = (f32[4,6,1,128]{3,2,1,0:T(1,128)S(1)}, f32[4,6,1,128]{3,2,1,0:T(1,128)S(1)}, u32[]{:S(2)}, u32[]{:S(2)}) collective-permute-start(f32[4,6,1,128]{3,2,1,0:T(1,128)S(1)} %get-tuple-element.116), channel_id=1, source_target_pairs={{0,1},{1,2},{2,3},{4,5},{5,6},{6,7},{8,9},{9,10},{10,11},{12,13},{... | collective-permute-start | bytes 36872 | tf_op jit(solution)/shard_map/ppermute | solution.py:20
  130.8 6.8 %collective-permute-start.16 = (f32[4,1,32,128]{3,2,1,0:T(8,128)S(1)}, f32[4,1,32,128]{3,2,1,0:T(8,128)S(1)}, u32[]{:S(2)}, u32[]{:S(2)}) collective-permute-start(f32[4,1,32,128]{3,2,1,0:T(8,128)S(1)} %get-tuple-element.144), channel_id=1, source_target_pairs={{0,4},{4,8},{8,12},{12,16},{16,20},{20,24},{24,28},{28,32},{32,36}... | collective-permute-start | bytes 196616 | tf_op jit(solution)/shard_map/ppermute | solution.py:20
  137.7 11.9 %collective-permute-start.19 = (f32[4,6,1,128]{3,2,1,0:T(1,128)S(1)}, f32[4,6,1,128]{3,2,1,0:T(1,128)S(1)}, u32[]{:S(2)}, u32[]{:S(2)}) collective-permute-start(f32[4,6,1,128]{3,2,1,0:T(1,128)S(1)} %get-tuple-element.115), channel_id=1, source_target_pairs={{1,0},{2,1},{3,2},{5,4},{6,5},{7,6},{9,8},{10,9},{11,10},{13,12},{... | collective-permute-start | bytes 36872 | tf_op jit(solution)/shard_map/ppermute | solution.py:23
  140.8 8.8 %collective-permute-start.18 = (f32[4,6,1,128]{3,2,1,0:T(1,128)S(1)}, f32[4,6,1,128]{3,2,1,0:T(1,128)S(1)}, u32[]{:S(2)}, u32[]{:S(2)}) collective-permute-start(f32[4,6,1,128]{3,2,1,0:T(1,128)S(1)} %get-tuple-element.114), channel_id=1, source_target_pairs={{0,1},{1,2},{2,3},{4,5},{5,6},{6,7},{8,9},{9,10},{10,11},{12,13},{... | collective-permute-start | bytes 36872 | tf_op jit(solution)/shard_map/ppermute | solution.py:20
  142.8 34.6 %collective-permute-start.32 = (f32[4,1,32,128]{3,2,1,0:T(8,128)}, f32[4,1,32,128]{3,2,1,0:T(8,128)S(1)}, u32[]{:S(2)}, u32[]{:S(2)}) collective-permute-start(f32[4,1,32,128]{3,2,1,0:T(8,128)} %get-tuple-element.137), channel_id=1, source_target_pairs={{0,4},{4,8},{8,12},{12,16},{16,20},{20,24},{24,28},{28,32},{32,36}... | collective-permute-start | bytes 196616 | tf_op jit(solution)/shard_map/ppermute | solution.py:20
  144.7 52.0 %collective-permute-start.33 = (f32[4,1,32,128]{3,2,1,0:T(8,128)}, f32[4,1,32,128]{3,2,1,0:T(8,128)}, u32[]{:S(2)}, u32[]{:S(2)}) collective-permute-start(f32[4,1,32,128]{3,2,1,0:T(8,128)} %get-tuple-element.136), channel_id=1, source_target_pairs={{4,0},{8,4},{12,8},{16,12},{20,16},{24,20},{28,24},{32,28},{36,32}... | collective-permute-start | bytes 196616 | tf_op jit(solution)/shard_map/ppermute | solution.py:23
  151.8 6.8 %collective-permute-start.20 = (f32[4,1,32,128]{3,2,1,0:T(8,128)S(1)}, f32[4,1,32,128]{3,2,1,0:T(8,128)S(1)}, u32[]{:S(2)}, u32[]{:S(2)}) collective-permute-start(f32[4,1,32,128]{3,2,1,0:T(8,128)S(1)} %get-tuple-element.142), channel_id=1, source_target_pairs={{0,4},{4,8},{8,12},{12,16},{16,20},{20,24},{24,28},{28,32},{32,36}... | collective-permute-start | bytes 196616 | tf_op jit(solution)/shard_map/ppermute | solution.py:20
  159.2 9.2 %collective-permute-start.23 = (f32[4,6,1,128]{3,2,1,0:T(1,128)}, f32[4,6,1,128]{3,2,1,0:T(1,128)}, u32[]{:S(2)}, u32[]{:S(2)}) collective-permute-start(f32[4,6,1,128]{3,2,1,0:T(1,128)} %get-tuple-element.113), channel_id=1, source_target_pairs={{1,0},{2,1},{3,2},{5,4},{6,5},{7,6},{9,8},{10,9},{11,10},{13,12},{... | collective-permute-start | bytes 36872 | tf_op jit(solution)/shard_map/ppermute | solution.py:23
  165.3 6.8 %collective-permute-start.22 = (f32[4,6,1,128]{3,2,1,0:T(1,128)}, f32[4,6,1,128]{3,2,1,0:T(1,128)}, u32[]{:S(2)}, u32[]{:S(2)}) collective-permute-start(f32[4,6,1,128]{3,2,1,0:T(1,128)} %get-tuple-element.112), channel_id=1, source_target_pairs={{0,1},{1,2},{2,3},{4,5},{5,6},{6,7},{8,9},{9,10},{10,11},{12,13},{... | collective-permute-start | bytes 36872 | tf_op jit(solution)/shard_map/ppermute | solution.py:20
  175.0 6.8 %collective-permute-start.24 = (f32[4,1,32,128]{3,2,1,0:T(8,128)S(1)}, f32[4,1,32,128]{3,2,1,0:T(8,128)S(1)}, u32[]{:S(2)}, u32[]{:S(2)}) collective-permute-start(f32[4,1,32,128]{3,2,1,0:T(8,128)S(1)} %get-tuple-element.140), channel_id=1, source_target_pairs={{0,4},{4,8},{8,12},{12,16},{16,20},{20,24},{24,28},{28,32},{32,36}... | collective-permute-start | bytes 196616 | tf_op jit(solution)/shard_map/ppermute | solution.py:20
  185.6 6.5 %collective-permute-start.26 = (f32[4,6,1,128]{3,2,1,0:T(1,128)S(1)}, f32[4,6,1,128]{3,2,1,0:T(1,128)S(1)}, u32[]{:S(2)}, u32[]{:S(2)}) collective-permute-start(f32[4,6,1,128]{3,2,1,0:T(1,128)S(1)} %get-tuple-element.110), channel_id=1, source_target_pairs={{0,1},{1,2},{2,3},{4,5},{5,6},{6,7},{8,9},{9,10},{10,11},{12,13},{... | collective-permute-start | bytes 36872 | tf_op jit(solution)/shard_map/ppermute | solution.py:20
  192.4 5.2 collective-permute-start.29
  194.3 6.8 %collective-permute-start.28 = (f32[4,1,32,128]{3,2,1,0:T(8,128)S(1)}, f32[4,1,32,128]{3,2,1,0:T(8,128)S(1)}, u32[]{:S(2)}, u32[]{:S(2)}) collective-permute-start(f32[4,1,32,128]{3,2,1,0:T(8,128)S(1)} %get-tuple-element.138), channel_id=1, source_target_pairs={{0,4},{4,8},{8,12},{12,16},{16,20},{20,24},{24,28},{28,32},{32,36}... | collective-permute-start | bytes 196616 | tf_op jit(solution)/shard_map/ppermute | solution.py:20
  201.1 11.2 %collective-permute-start.31 = (f32[4,6,1,128]{3,2,1,0:T(1,128)S(1)}, f32[4,6,1,128]{3,2,1,0:T(1,128)S(1)}, u32[]{:S(2)}, u32[]{:S(2)}) collective-permute-start(f32[4,6,1,128]{3,2,1,0:T(1,128)S(1)} %get-tuple-element.109), channel_id=1, source_target_pairs={{1,0},{2,1},{3,2},{5,4},{6,5},{7,6},{9,8},{10,9},{11,10},{13,12},{... | collective-permute-start | bytes 36872 | tf_op jit(solution)/shard_map/ppermute | solution.py:23
  204.3 8.1 %collective-permute-start.30 = (f32[4,6,1,128]{3,2,1,0:T(1,128)S(1)}, f32[4,6,1,128]{3,2,1,0:T(1,128)S(1)}, u32[]{:S(2)}, u32[]{:S(2)}) collective-permute-start(f32[4,6,1,128]{3,2,1,0:T(1,128)S(1)} %get-tuple-element.108), channel_id=1, source_target_pairs={{0,1},{1,2},{2,3},{4,5},{5,6},{6,7},{8,9},{9,10},{10,11},{12,13},{... | collective-permute-start | bytes 36872 | tf_op jit(solution)/shard_map/ppermute | solution.py:20
  205.6 147.3 %collective-permute-start.35 = (f32[4,6,1,128]{3,2,1,0:T(1,128)S(1)}, f32[4,6,1,128]{3,2,1,0:T(1,128)S(1)}, u32[]{:S(2)}, u32[]{:S(2)}) collective-permute-start(f32[4,6,1,128]{3,2,1,0:T(1,128)S(1)} %get-tuple-element.107), channel_id=1, source_target_pairs={{1,0},{2,1},{3,2},{5,4},{6,5},{7,6},{9,8},{10,9},{11,10},{13,12},{... | collective-permute-start | bytes 36872 | tf_op jit(solution)/shard_map/ppermute | solution.py:23
  211.1 141.8 %collective-permute-start.34 = (f32[4,6,1,128]{3,2,1,0:T(1,128)S(1)}, f32[4,6,1,128]{3,2,1,0:T(1,128)S(1)}, u32[]{:S(2)}, u32[]{:S(2)}) collective-permute-start(f32[4,6,1,128]{3,2,1,0:T(1,128)S(1)} %get-tuple-element.106), channel_id=1, source_target_pairs={{0,1},{1,2},{2,3},{4,5},{5,6},{6,7},{8,9},{9,10},{10,11},{12,13},{... | collective-permute-start | bytes 36872 | tf_op jit(solution)/shard_map/ppermute | solution.py:20
  354.1 5.9 %collective-permute-start.37 = (f32[4,1,32,128]{3,2,1,0:T(8,128)S(1)}, f32[4,1,32,128]{3,2,1,0:T(8,128)S(1)}, u32[]{:S(2)}, u32[]{:S(2)}) collective-permute-start(f32[4,1,32,128]{3,2,1,0:T(8,128)S(1)} %get-tuple-element.135), channel_id=1, source_target_pairs={{4,0},{8,4},{12,8},{16,12},{20,16},{24,20},{28,24},{32,28},{36,32}... | collective-permute-start | bytes 196616 | tf_op jit(solution)/shard_map/ppermute | solution.py:23
  358.0 6.8 %collective-permute-start.36 = (f32[4,1,32,128]{3,2,1,0:T(8,128)S(1)}, f32[4,1,32,128]{3,2,1,0:T(8,128)S(1)}, u32[]{:S(2)}, u32[]{:S(2)}) collective-permute-start(f32[4,1,32,128]{3,2,1,0:T(8,128)S(1)} %get-tuple-element.134), channel_id=1, source_target_pairs={{0,4},{4,8},{8,12},{12,16},{16,20},{20,24},{24,28},{28,32},{32,36}... | collective-permute-start | bytes 196616 | tf_op jit(solution)/shard_map/ppermute | solution.py:20
  368.4 6.5 %collective-permute-start.38 = (f32[4,6,1,128]{3,2,1,0:T(1,128)S(1)}, f32[4,6,1,128]{3,2,1,0:T(1,128)S(1)}, u32[]{:S(2)}, u32[]{:S(2)}) collective-permute-start(f32[4,6,1,128]{3,2,1,0:T(1,128)S(1)} %get-tuple-element.104), channel_id=1, source_target_pairs={{0,1},{1,2},{2,3},{4,5},{5,6},{6,7},{8,9},{9,10},{10,11},{12,13},{... | collective-permute-start | bytes 36872 | tf_op jit(solution)/shard_map/ppermute | solution.py:20
  377.1 6.8 %collective-permute-start.40 = (f32[4,1,32,128]{3,2,1,0:T(8,128)S(1)}, f32[4,1,32,128]{3,2,1,0:T(8,128)S(1)}, u32[]{:S(2)}, u32[]{:S(2)}) collective-permute-start(f32[4,1,32,128]{3,2,1,0:T(8,128)S(1)} %get-tuple-element.132), channel_id=1, source_target_pairs={{0,4},{4,8},{8,12},{12,16},{16,20},{20,24},{24,28},{28,32},{32,36}... | collective-permute-start | bytes 196616 | tf_op jit(solution)/shard_map/ppermute | solution.py:20
  383.9 6.2 %collective-permute-start.43 = (f32[4,6,1,128]{3,2,1,0:T(1,128)S(1)}, f32[4,6,1,128]{3,2,1,0:T(1,128)S(1)}, u32[]{:S(2)}, u32[]{:S(2)}) collective-permute-start(f32[4,6,1,128]{3,2,1,0:T(1,128)S(1)} %get-tuple-element.103), channel_id=1, source_target_pairs={{1,0},{2,1},{3,2},{5,4},{6,5},{7,6},{9,8},{10,9},{11,10},{13,12},{... | collective-permute-start | bytes 36872 | tf_op jit(solution)/shard_map/ppermute | solution.py:23
  388.8 6.5 %collective-permute-start.42 = (f32[4,6,1,128]{3,2,1,0:T(1,128)S(1)}, f32[4,6,1,128]{3,2,1,0:T(1,128)S(1)}, u32[]{:S(2)}, u32[]{:S(2)}) collective-permute-start(f32[4,6,1,128]{3,2,1,0:T(1,128)S(1)} %get-tuple-element.102), channel_id=1, source_target_pairs={{0,1},{1,2},{2,3},{4,5},{5,6},{6,7},{8,9},{9,10},{10,11},{12,13},{... | collective-permute-start | bytes 36872 | tf_op jit(solution)/shard_map/ppermute | solution.py:20
  397.5 6.8 %collective-permute-start.44 = (f32[4,1,32,128]{3,2,1,0:T(8,128)S(1)}, f32[4,1,32,128]{3,2,1,0:T(8,128)S(1)}, u32[]{:S(2)}, u32[]{:S(2)}) collective-permute-start(f32[4,1,32,128]{3,2,1,0:T(8,128)S(1)} %get-tuple-element.130), channel_id=1, source_target_pairs={{0,4},{4,8},{8,12},{12,16},{16,20},{20,24},{24,28},{28,32},{32,36}... | collective-permute-start | bytes 196616 | tf_op jit(solution)/shard_map/ppermute | solution.py:20
  404.3 7.1 %collective-permute-start.47 = (f32[4,6,1,128]{3,2,1,0:T(1,128)S(1)}, f32[4,6,1,128]{3,2,1,0:T(1,128)S(1)}, u32[]{:S(2)}, u32[]{:S(2)}) collective-permute-start(f32[4,6,1,128]{3,2,1,0:T(1,128)S(1)} %get-tuple-element.101), channel_id=1, source_target_pairs={{1,0},{2,1},{3,2},{5,4},{6,5},{7,6},{9,8},{10,9},{11,10},{13,12},{... | collective-permute-start | bytes 36872 | tf_op jit(solution)/shard_map/ppermute | solution.py:23
  409.9 6.5 %collective-permute-start.46 = (f32[4,6,1,128]{3,2,1,0:T(1,128)S(1)}, f32[4,6,1,128]{3,2,1,0:T(1,128)S(1)}, u32[]{:S(2)}, u32[]{:S(2)}) collective-permute-start(f32[4,6,1,128]{3,2,1,0:T(1,128)S(1)} %get-tuple-element.100), channel_id=1, source_target_pairs={{0,1},{1,2},{2,3},{4,5},{5,6},{6,7},{8,9},{9,10},{10,11},{12,13},{... | collective-permute-start | bytes 36872 | tf_op jit(solution)/shard_map/ppermute | solution.py:20
  418.6 6.8 %collective-permute-start.48 = (f32[4,1,32,128]{3,2,1,0:T(8,128)S(1)}, f32[4,1,32,128]{3,2,1,0:T(8,128)S(1)}, u32[]{:S(2)}, u32[]{:S(2)}) collective-permute-start(f32[4,1,32,128]{3,2,1,0:T(8,128)S(1)} %get-tuple-element.128), channel_id=1, source_target_pairs={{0,4},{4,8},{8,12},{12,16},{16,20},{20,24},{24,28},{28,32},{32,36}... | collective-permute-start | bytes 196616 | tf_op jit(solution)/shard_map/ppermute | solution.py:20
  428.6 6.5 %collective-permute-start.50 = (f32[4,6,1,128]{3,2,1,0:T(1,128)S(1)}, f32[4,6,1,128]{3,2,1,0:T(1,128)S(1)}, u32[]{:S(2)}, u32[]{:S(2)}) collective-permute-start(f32[4,6,1,128]{3,2,1,0:T(1,128)S(1)} %get-tuple-element.98), channel_id=1, source_target_pairs={{0,1},{1,2},{2,3},{4,5},{5,6},{6,7},{8,9},{9,10},{10,11},{12,13},{... | collective-permute-start | bytes 36872 | tf_op jit(solution)/shard_map/ppermute | solution.py:20
  437.3 6.8 %collective-permute-start.52 = (f32[4,1,32,128]{3,2,1,0:T(8,128)S(1)}, f32[4,1,32,128]{3,2,1,0:T(8,128)S(1)}, u32[]{:S(2)}, u32[]{:S(2)}) collective-permute-start(f32[4,1,32,128]{3,2,1,0:T(8,128)S(1)} %get-tuple-element.126), channel_id=1, source_target_pairs={{0,4},{4,8},{8,12},{12,16},{16,20},{20,24},{24,28},{28,32},{32,36}... | collective-permute-start | bytes 196616 | tf_op jit(solution)/shard_map/ppermute | solution.py:20
  447.3 6.5 %collective-permute-start.54 = (f32[4,6,1,128]{3,2,1,0:T(1,128)S(1)}, f32[4,6,1,128]{3,2,1,0:T(1,128)S(1)}, u32[]{:S(2)}, u32[]{:S(2)}) collective-permute-start(f32[4,6,1,128]{3,2,1,0:T(1,128)S(1)} %get-tuple-element.96), channel_id=1, source_target_pairs={{0,1},{1,2},{2,3},{4,5},{5,6},{6,7},{8,9},{9,10},{10,11},{12,13},{... | collective-permute-start | bytes 36872 | tf_op jit(solution)/shard_map/ppermute | solution.py:20
  456.0 6.8 %collective-permute-start.56 = (f32[4,1,32,128]{3,2,1,0:T(8,128)S(1)}, f32[4,1,32,128]{3,2,1,0:T(8,128)S(1)}, u32[]{:S(2)}, u32[]{:S(2)}) collective-permute-start(f32[4,1,32,128]{3,2,1,0:T(8,128)S(1)} %get-tuple-element.124), channel_id=1, source_target_pairs={{0,4},{4,8},{8,12},{12,16},{16,20},{20,24},{24,28},{28,32},{32,36}... | collective-permute-start | bytes 196616 | tf_op jit(solution)/shard_map/ppermute | solution.py:20
  466.0 6.5 %collective-permute-start.58 = (f32[4,6,1,128]{3,2,1,0:T(1,128)S(1)}, f32[4,6,1,128]{3,2,1,0:T(1,128)S(1)}, u32[]{:S(2)}, u32[]{:S(2)}) collective-permute-start(f32[4,6,1,128]{3,2,1,0:T(1,128)S(1)} %get-tuple-element.94), channel_id=1, source_target_pairs={{0,1},{1,2},{2,3},{4,5},{5,6},{6,7},{8,9},{9,10},{10,11},{12,13},{... | collective-permute-start | bytes 36872 | tf_op jit(solution)/shard_map/ppermute | solution.py:20
  474.9 7.6 %collective-permute-start.60 = (f32[8,1,32,128]{3,2,1,0:T(8,128)S(1)}, f32[8,1,32,128]{3,2,1,0:T(8,128)S(1)}, u32[]{:S(2)}, u32[]{:S(2)}) collective-permute-start(f32[8,1,32,128]{3,2,1,0:T(8,128)S(1)} %get-tuple-element.90), channel_id=1, source_target_pairs={{0,4},{4,8},{8,12},{12,16},{16,20},{20,24},{24,28},{28,32},{32,36}... | collective-permute-start | bytes 393224 | tf_op jit(solution)/shard_map/ppermute | solution.py:20
  482.5 5.3 %collective-permute-start.63 = (f32[8,6,1,128]{3,2,1,0:T(1,128)S(1)}, f32[8,6,1,128]{3,2,1,0:T(1,128)S(1)}, u32[]{:S(2)}, u32[]{:S(2)}) collective-permute-start(f32[8,6,1,128]{3,2,1,0:T(1,128)S(1)} %get-tuple-element.83), channel_id=1, source_target_pairs={{1,0},{2,1},{3,2},{5,4},{6,5},{7,6},{9,8},{10,9},{11,10},{13,12},{... | collective-permute-start | bytes 73736 | tf_op jit(solution)/shard_map/ppermute | solution.py:23
  485.8 7.1 %collective-permute-start.62 = (f32[8,6,1,128]{3,2,1,0:T(1,128)S(1)}, f32[8,6,1,128]{3,2,1,0:T(1,128)S(1)}, u32[]{:S(2)}, u32[]{:S(2)}) collective-permute-start(f32[8,6,1,128]{3,2,1,0:T(1,128)S(1)} %get-tuple-element.82), channel_id=1, source_target_pairs={{0,1},{1,2},{2,3},{4,5},{5,6},{6,7},{8,9},{9,10},{10,11},{12,13},{... | collective-permute-start | bytes 73736 | tf_op jit(solution)/shard_map/ppermute | solution.py:20
  (37 other events, 753.6 us)
